TPU v7x, 32 devices: a whole 2x2x4 slice. The times are simulated.
32 devices in a mesh: chan: 4 (over z), ctx: 8 (over y, x, core).
Axes of the slice: x: 2, y: 2, z: 4, core: 2. Of those that a mesh axis runs over, the one named last changes fastest.
Arguments:
- projected: bfloat16 [8, 512, 3, 4096], P('ctx', 'chan'), may hold values from -6 to 6
- short_taps: bfloat16 [3, 3, 4096], replicated, may hold values from -3 to 3
- long_filter: float32 [4096, 16], P('ctx', 'chan'), may hold values from -0.09375 to 0.09375
- skip_gain: float32 [4096], P('chan'), may hold values from -4 to 4
Outputs:
- gated: bfloat16 [4096, 4096], P('ctx', 'chan')
All inputs are finite; a program needn't handle non-finite values.
Results may differ from a plain program's by a relative error of at most 0.0064.
Values may be sent and summed in bfloat16 or wider, within the bound.
A program may use at most 128 MiB of HBM per device.

v0:
```python
import functools
import math

import jax
import jax.numpy as jnp
from jax import lax
from jax.experimental import pallas as pl
from jax.experimental.pallas import tpu as pltpu
from jax.sharding import PartitionSpec as P

TAPS = 3


PRECISE = lax.Precision.HIGHEST


def passed_along(value, axis, by):
    count = lax.axis_size(axis)
    pairs = [(i, i + by) for i in range(count) if 0 <= i + by < count]
    return lax.ppermute(value, axis, pairs)


def counting(length):
    return jnp.arange(length, dtype=jnp.int32)


def phases(first, second, length):
    turned = first[:, None] * second[None, :] % length
    angles = turned.astype(jnp.float32) * (2.0 * math.pi / length)
    return (jnp.cos(angles), jnp.sin(angles))


def rotate(real_part, imag_part, cosines, sines, direction):
    return (
        real_part * cosines - direction * imag_part * sines,
        imag_part * cosines + direction * real_part * sines,
    )


def complex_mix(pattern, cosines, sines, real_part, imag_part, direction):
    cos_real = jnp.einsum(pattern, cosines, real_part, precision=PRECISE)
    sin_real = jnp.einsum(pattern, sines, real_part, precision=PRECISE)
    if imag_part is None:
        return (cos_real, direction * sin_real)
    cos_imag = jnp.einsum(pattern, cosines, imag_part, precision=PRECISE)
    sin_imag = jnp.einsum(pattern, sines, imag_part, precision=PRECISE)
    return (cos_real - direction * sin_imag, cos_imag + direction * sin_real)


def leading_factor(length):
    chosen = 1
    for option in range(1, math.isqrt(length) + 1):
        if length % option == 0:
            chosen = option
    return chosen


def local_tables(first, second):
    cos_one, sin_one = phases(counting(first), counting(first), first)
    cos_two, sin_two = phases(counting(second), counting(second), second)
    cos_mid, sin_mid = phases(counting(first), counting(second), first * second)
    return (
        cos_one,
        sin_one,
        cos_two,
        sin_two,
        cos_mid[None, :, :, None],
        sin_mid[None, :, :, None],
    )


def inner_forward(real_part, imag_part):
    leading, length, columns = real_part.shape
    first = leading_factor(length)
    second = length // first
    cos_one, sin_one, cos_two, sin_two, cos_mid, sin_mid = local_tables(first, second)
    real_part = real_part.reshape(leading, first, second, columns)
    if imag_part is not None:
        imag_part = imag_part.reshape(leading, first, second, columns)
    real_part, imag_part = complex_mix(
        "bk,akjx->abjx", cos_one, sin_one, real_part, imag_part, -1.0
    )
    real_part, imag_part = rotate(real_part, imag_part, cos_mid, sin_mid, -1.0)
    return complex_mix("ej,abjx->abex", cos_two, sin_two, real_part, imag_part, -1.0)


def inner_inverse(real_part, imag_part):
    leading, first, second, columns = real_part.shape
    cos_one, sin_one, cos_two, sin_two, cos_mid, sin_mid = local_tables(first, second)
    real_part, imag_part = complex_mix("ej,abjx->abex", cos_two, sin_two, real_part, imag_part, 1.0)
    real_part, imag_part = rotate(real_part, imag_part, cos_mid, sin_mid, 1.0)
    real_part, imag_part = complex_mix("kb,abjx->akjx", cos_one, sin_one, real_part, imag_part, 1.0)
    return (
        real_part.reshape(leading, first * second, columns),
        imag_part.reshape(leading, first * second, columns),
    )


def featurize(earlier, own_rows, filter_taps):
    lag_rows = earlier.shape[0]
    length = own_rows.shape[0]
    extended = jnp.concatenate([earlier, own_rows], axis=0).astype(jnp.float32)
    weights = filter_taps.astype(jnp.float32)
    summed = weights[0] * extended[lag_rows : lag_rows + length]
    for offset in range(1, weights.shape[0]):
        summed = summed + weights[offset] * extended[lag_rows - offset : lag_rows - offset + length]
    queries = lax.optimization_barrier(summed[:, 0].astype(jnp.bfloat16))
    product = (summed[:, 1] * summed[:, 2]).astype(jnp.bfloat16)
    return (queries, product)


def whole_transform(real_part, imag_part):
    zeros = jnp.zeros_like(real_part)
    padded_real = jnp.concatenate([real_part, zeros], axis=0)[None]
    padded_imag = None
    if imag_part is not None:
        padded_imag = jnp.concatenate([imag_part, zeros], axis=0)[None]
    return inner_forward(padded_real, padded_imag)


def local_convolve(signal, filters, gains_here, position, per_group):
    length, columns = signal.shape
    groups_here = filters.shape[1]
    first_channel = position * columns
    pairs = signal.reshape(length, columns // 2, 2)
    real_in = pairs[:, :, 0]
    imag_in = pairs[:, :, 1]
    owners = (first_channel + 2 * counting(columns // 2)) // per_group
    selector = (counting(groups_here)[:, None] == owners[None, :]).astype(jnp.float32)
    filt_real, filt_imag = whole_transform(filters, None)
    filt_real = jnp.einsum("abex,xc->abec", filt_real, selector, precision=PRECISE)
    filt_imag = jnp.einsum("abex,xc->abec", filt_imag, selector, precision=PRECISE)
    sig_real, sig_imag = whole_transform(real_in, imag_in)
    prod_real = sig_real * filt_real - sig_imag * filt_imag
    prod_imag = sig_real * filt_imag + sig_imag * filt_real
    back_real, back_imag = inner_inverse(prod_real, prod_imag)
    inverse_scale = 1.0 / (2 * length)
    conv_real = back_real[0, :length] * inverse_scale
    conv_imag = back_imag[0, :length] * inverse_scale
    convolved = jnp.stack([conv_real, conv_imag], axis=2).reshape(length, columns)
    return convolved + gains_here * signal


def by_transform(projected, short_taps, long_filter, skip_gain):
    devices = lax.axis_size("ctx")
    position = lax.axis_index("ctx")
    channel_slot = lax.axis_index("chan")
    channels = skip_gain.shape[0]
    groups_here = long_filter.shape[1]
    per_group = channels // groups_here
    regrouped = lax.all_to_all(projected, "chan", split_axis=3, concat_axis=1, tiled=True)[0]
    taps_here = lax.dynamic_slice_in_dim(short_taps, channel_slot * channels, channels, 2)
    last_rows = regrouped[regrouped.shape[0] - (TAPS - 1) :]
    earlier = passed_along(last_rows, "ctx", 1)
    queries, product = featurize(earlier, regrouped, taps_here)
    kv_seq = lax.all_to_all(product[None], "ctx", split_axis=2, concat_axis=0, tiled=True)
    block_rows = kv_seq.shape[1]
    columns = kv_seq.shape[2]
    signal = kv_seq.reshape(devices * block_rows, columns).astype(jnp.float32)
    filters = lax.all_gather(long_filter, "ctx", axis=0, tiled=True)
    gains_here = lax.dynamic_slice_in_dim(skip_gain, position * columns, columns, 0)
    mixed = local_convolve(signal, filters, gains_here, position, per_group).astype(jnp.bfloat16)
    mixed = mixed.reshape(devices, block_rows, columns)
    mixed_rows = lax.all_to_all(mixed, "ctx", split_axis=0, concat_axis=2, tiled=True)[0]
    return (queries.astype(jnp.float32) * mixed_rows.astype(jnp.float32)).astype(jnp.bfloat16)


TILE = 256


def exchange_kernel(
    query_ref,
    kv_ref,
    lags_ref,
    gain_ref,
    out_ref,
    query_rows,
    kv_rows,
    kv_seq,
    mixed_out,
    mixed_in,
    toeplitz,
    kv_send,
    kv_recv,
    query_send,
    query_recv,
    seq_send,
    seq_recv,
    back_send,
    back_recv,
):
    chans = lax.axis_size("chan")
    blocks = lax.axis_size("ctx")
    my_chan = lax.axis_index("chan")
    my_block = lax.axis_index("ctx")
    rows = kv_ref.shape[0]
    width = kv_rows.shape[1]
    columns = kv_seq.shape[1]
    block_rows = rows * chans

    def other_chan(step):
        return lax.rem(my_chan + step + chans, chans)

    def other_block(step):
        return lax.rem(my_block + step + blocks, blocks)

    barrier = pltpu.get_barrier_semaphore()
    for step in range(1, chans):
        pl.semaphore_signal(barrier, inc=1, device_id={"chan": other_chan(step)})
    for step in range(1, blocks):
        pl.semaphore_signal(barrier, inc=1, device_id={"ctx": other_block(step)})
    pl.semaphore_wait(barrier, chans + blocks - 2)

    def lanes(index, size):
        return pl.ds(pl.multiple_of(index * size, size), size)

    def over_chan(source, target, send, recv, step):
        to = other_chan(step)
        return pltpu.make_async_remote_copy(
            src_ref=source.at[:, lanes(to, width)],
            dst_ref=target.at[lanes(my_chan, rows), :],
            send_sem=send.at[step],
            recv_sem=recv.at[step],
            device_id={"chan": to},
        )

    kv_copies = [over_chan(kv_ref, kv_rows, kv_send, kv_recv, step) for step in range(1, chans)]
    query_copies = [
        over_chan(query_ref, query_rows, query_send, query_recv, step) for step in range(1, chans)
    ]
    for copy in kv_copies:
        copy.start()
    kv_rows[lanes(my_chan, rows), :] = kv_ref[:, lanes(my_chan, width)]
    query_rows[lanes(my_chan, rows), :] = query_ref[:, lanes(my_chan, width)]

    seq_copies = []

    def forward(step):
        origin = other_chan(-step)
        here = lanes(origin, rows)
        there = lanes(my_block * chans + origin, rows)
        for hop in range(1, blocks):
            to = other_block(hop)
            copy = pltpu.make_async_remote_copy(
                src_ref=kv_rows.at[here, lanes(to, columns)],
                dst_ref=kv_seq.at[there, :],
                send_sem=seq_send.at[step, hop],
                recv_sem=seq_recv.at[step, hop],
                device_id={"ctx": to},
            )
            copy.start()
            seq_copies.append(copy)
        kv_seq[there, :] = kv_rows[here, lanes(my_block, columns)]

    forward(0)

    toeplitz[0:TILE, :] = jnp.zeros((TILE, TILE), jnp.bfloat16)
    length = kv_seq.shape[0]
    for tile in range(length // TILE):
        first = length - TILE - tile * TILE
        window = jnp.broadcast_to(lags_ref[:, first : first + 2 * TILE], (TILE, 2 * TILE))
        turned = pltpu.roll(window, TILE + 1, 1, stride=1, stride_axis=0)
        toeplitz[(tile + 1) * TILE : (tile + 2) * TILE, :] = turned[:, :TILE].astype(jnp.bfloat16)

    for step in range(1, chans):
        kv_copies[step - 1].wait_recv()
        forward(step)
    for copy in query_copies:
        copy.start()
    for copy in seq_copies:
        copy.wait_recv()

    gain = gain_ref[...]

    def returning(hop):
        to = other_block(hop)
        return pltpu.make_async_remote_copy(
            src_ref=mixed_out.at[lanes(to, block_rows), :],
            dst_ref=mixed_in.at[:, lanes(my_block, columns)],
            send_sem=back_send.at[hop],
            recv_sem=back_recv.at[hop],
            device_id={"ctx": to},
        )

    def convolve(block):
        def term(step, total):
            later = block * block_rows - step * TILE + TILE
            left = toeplitz[pl.ds(pl.multiple_of(later, TILE), block_rows), :]
            right = kv_seq[lanes(step, TILE), :]
            return total + jnp.dot(left, right, preferred_element_type=jnp.float32)

        start = jnp.zeros((block_rows, columns), jnp.float32)
        total = lax.fori_loop(0, (block + 1) * (block_rows // TILE), term, start)
        here = lanes(block, block_rows)
        mixed_out[here, :] = (total + gain * kv_seq[here, :].astype(jnp.float32)).astype(jnp.bfloat16)

    back_copies = []
    for hop in range(1, blocks):
        convolve(other_block(hop))
        copy = returning(hop)
        copy.start()
        back_copies.append(copy)
    convolve(my_block)
    mixed_in[:, lanes(my_block, columns)] = mixed_out[lanes(my_block, block_rows), :]

    for copy in query_copies:
        copy.wait_recv()

    def gate(hop):
        here = lanes(other_block(-hop), columns)
        product = query_rows[:, here].astype(jnp.float32) * mixed_in[:, here].astype(jnp.float32)
        out_ref[:, here] = product.astype(jnp.bfloat16)

    gate(0)
    for hop in range(1, blocks):
        back_copies[hop - 1].wait_recv()
        gate(hop)
    for copy in kv_copies + query_copies + seq_copies + back_copies:
        copy.wait_send()


def by_products(projected, short_taps, long_filter, skip_gain):
    chans = lax.axis_size("chan")
    blocks = lax.axis_size("ctx")
    my_chan = lax.axis_index("chan")
    my_block = lax.axis_index("ctx")
    own = projected[0]
    rows, _, channels = own.shape
    width = skip_gain.shape[0]
    columns = width // blocks
    per_group = width // long_filter.shape[1]
    length = rows * chans * blocks
    last = own[rows - (TAPS - 1) :]
    pairs = []
    for at in range(blocks * chans - 1):
        source = (at % chans) * blocks + at // chans
        after = at + 1
        pairs.append((source, (after % chans) * blocks + after // chans))
    earlier = lax.ppermute(last, ("chan", "ctx"), pairs)
    queries, product = featurize(earlier, own, short_taps)

    group = my_block * columns // per_group
    lags = lax.all_gather(long_filter.T, "ctx", axis=1, tiled=True)
    lags = lax.dynamic_slice_in_dim(lags, group, 1, 0)
    lags = jnp.pad(jnp.flip(lags, 1), ((0, 0), (0, TILE)))
    gains = lax.dynamic_slice_in_dim(skip_gain, my_block * columns, columns, 0)[None]

    block_rows = rows * chans
    vmem = pl.BlockSpec(memory_space=pltpu.VMEM)
    dma = pltpu.SemaphoreType.DMA
    return pl.pallas_call(
        exchange_kernel,
        out_shape=jax.ShapeDtypeStruct((block_rows, width), jnp.bfloat16),
        in_specs=[vmem] * 4,
        out_specs=vmem,
        scratch_shapes=[
            pltpu.VMEM((block_rows, width), jnp.bfloat16),
            pltpu.VMEM((block_rows, width), jnp.bfloat16),
            pltpu.VMEM((length, columns), jnp.bfloat16),
            pltpu.VMEM((length, columns), jnp.bfloat16),
            pltpu.VMEM((block_rows, width), jnp.bfloat16),
            pltpu.VMEM((length + TILE, TILE), jnp.bfloat16),
            dma((chans,)),
            dma((chans,)),
            dma((chans,)),
            dma((chans,)),
            dma((chans, blocks)),
            dma((chans, blocks)),
            dma((blocks,)),
            dma((blocks,)),
        ],
        compiler_params=pltpu.CompilerParams(
            collective_id=0, has_side_effects=True, vmem_limit_bytes=40 * 1024 * 1024
        ),
    )(queries, product, lags, gains)


def local(projected, short_taps, long_filter, skip_gain):
    chans = lax.axis_size("chan")
    blocks = lax.axis_size("ctx")
    rows = projected.shape[1]
    width = skip_gain.shape[0]
    columns = width // blocks
    per_group = width // long_filter.shape[1]
    fits = columns % 128 == 0 and per_group % columns == 0
    fits = fits and rows % 16 == 0 and rows * chans % TILE == 0
    if fits:
        return by_products(projected, short_taps, long_filter, skip_gain)
    return by_transform(projected, short_taps, long_filter, skip_gain)


def solution(mesh):
    placed = (P("ctx", "chan", None, None), P(), P("ctx", "chan"), P("chan"))
    return jax.shard_map(
        local, mesh=mesh, in_specs=placed, out_specs=P("ctx", "chan"), check_vma=False
    )
```

profile of v0, /device:TPU:31, one launch (start us, length us, event | category | flops | bytes accessed | tf_op | source)
XLA Modules:
  0.0 79.9 jit_solution(10126987558103406149)
XLA Ops:
  0.0 0.0 copy-start
  0.0 1.0 %slice_bitcast_fusion.3 = bf16[2,3,4096]{2,0,1:T(2,128)(2,1)S(1)} fusion(bf16[1,128,3,4096]{3,1,2,0:T(8,128)(2,1)} %param.4), kind=kLoop, calls=%fused_computation.14 | loop fusion | bytes 98304 | tf_op jit(solution)/shard_map/slice | solution.py:333
  1.0 1.3 %collective-permute-start = (bf16[2,3,4096]{2,0,1:T(2,128)(2,1)S(1)}, bf16[2,3,4096]{2,0,1:T(2,128)(2,1)S(1)}, u32[]{:S(2)}, u32[]{:S(2)}) collective-permute-start(bf16[2,3,4096]{2,0,1:T(2,128)(2,1)S(1)} %slice_bitcast_fusion.3), channel_id=1, source_target_pairs={{0,8},{8,16},{16,24},{24,1},{1,9},{9,17},{17,25},{25,2},{2,10},{10... | collective-permute-start | bytes 147464 | tf_op jit(solution)/shard_map/ppermute | solution.py:339
  2.3 0.9 %convert_element_type.17 = f32[3,3,4096]{2,1,0:T(4,128)S(1)} convert(bf16[3,3,4096]{2,1,0:T(4,128)(2,1)} %param.5) | non-fusion elementwise | flops 36864 | bytes 221184 | tf_op jit(solution)/shard_map/convert_element_type | solution.py:103
  3.3 9.5 %all_gather.3 = f32[4,4096]{1,0:T(4,128)S(1)} all-gather(f32[4,512]{1,0:T(4,128)} %bitcast.17), channel_id=1, replica_groups=mesh['chan'=4,'ctx'=8] {'ctx'}, dimensions={1}, use_global_device_ids=true | all-gather | bytes 73728 | tf_op jit(solution)/shard_map/all_gather | solution.py:343
  12.8 0.0 copy-done
  12.8 0.1 dynamic-slice_bitcast_fusion.gain_ref
  12.9 2.8 %rev.4 = f32[1,4096]{1,0:T(1,128)S(1)} reverse(f32[1,4096]{1,0:T(1,128)S(1)} %constant_dynamic-slice_fusion), dimensions={1} | reverse | bytes 32768 | tf_op jit(solution)/shard_map/jit(_flip)/rev | solution.py:345
  15.7 0.0 collective-permute-done
  15.7 2.9 %maximum_convert_fusion = f32[130,3,4096]{2,0,1:T(8,128)S(1)} fusion(bf16[128,3,4096]{2,0,1:T(8,128)(2,1)} %bitcast.16, bf16[2,3,4096]{2,0,1:T(2,128)(2,1)S(1)} %collective-permute-done), kind=kLoop, calls=%fused_computation.5 | loop fusion | flops 6389760 | bytes 9584640 | tf_op jit(solution)/shard_map/convert_element_type | solution.py:102
  18.6 1.9 %fusion = f32[128,3,4096]{2,0,1:T(8,128)S(1)} fusion(f32[130,3,4096]{2,0,1:T(8,128)S(1)} %maximum_convert_fusion, f32[3,4096]{1,0:T(4,128)S(1)} %get-tuple-element.6, f32[3,4096]{1,0:T(4,128)S(1)} %get-tuple-element.7, f32[3,4096]{1,0:T(4,128)S(1)} %get-tuple-element.5), kind=kLoop, calls=%fused_computation.1 | loop fusion | flops 7864320 | bytes 25313280 | tf_op jit(solution)/shard_map/add | solution.py:106
  20.5 0.1 fusion.3.query_ref
  20.6 0.2 fusion.4.kv_ref
  20.8 58.1 %shard_map.46 = bf16[512,1024]{1,0:T(8,128)(2,1)S(1)} custom-call(bf16[128,4096]{1,0:T(8,128)(2,1)S(1)} %fusion.3.query_ref, bf16[128,4096]{1,0:T(8,128)(2,1)S(1)} %fusion.4.kv_ref, f32[1,4352]{1,0:T(1,128)S(1)} %pad.4.lags_ref, f32[1,128]{1,0:T(1,128)S(1)} %dynamic-slice_bitcast_fusion.gain_ref), custom_call_target="tpu_custom_call" | custom-call | tf_op jit(solution)/shard_map/pallas_call | solution.py:351
  78.9 1.0 %copy.6 = bf16[512,1024]{1,0:T(8,128)(2,1)} copy(bf16[512,1024]{1,0:T(8,128)(2,1)S(1)} %shard_map.46) | data formatting | bytes 2097152
  (3 shorter events, 0.1 us)
Async XLA Ops:
  0.0 12.8 %copy-start = (f32[1024]{0:T(1024)S(1)}, f32[1024]{0:T(1024)}, u32[]{:S(2)}) copy-start(f32[1024]{0:T(1024)} %param.7) | copy-start | bytes 12292
  1.0 14.7 %collective-permute-start = (bf16[2,3,4096]{2,0,1:T(2,128)(2,1)S(1)}, bf16[2,3,4096]{2,0,1:T(2,128)(2,1)S(1)}, u32[]{:S(2)}, u32[]{:S(2)}) collective-permute-start(bf16[2,3,4096]{2,0,1:T(2,128)(2,1)S(1)} %slice_bitcast_fusion.3), channel_id=1, source_target_pairs={{0,8},{8,16},{16,24},{24,1},{1,9},{9,17},{17,25},{25,2},{2,10},{10... | collective-permute-start | bytes 147464 | tf_op jit(solution)/shard_map/ppermute | solution.py:339
where the time goes:
time: 80.2 us; the launch traced here: 79.9 us
  Pallas kernels  58.1 us (72%)
  blocking collectives  9.51 us (12%)
  other arithmetic  5.9 us (7%)
  local copies, waits for them, and re-layouts  5.02 us (6%)
  starting transfers between devices  1.29 us (2%)
    pallas_call x1, Pallas kernels, by_products(): pl.pallas_call(exchange_kernel, out_shape=jax.ShapeDtypeStruct((block_row...  58.1 us
    all_gather x1, blocking collectives, by_products(): lags = lax.all_gather(long_filter.T, 'ctx', axis=1, tiled=True)  9.51 us
    convert_element_type x1, other arithmetic, featurize(): extended = jnp.concatenate([earlier, own_rows], axis=0).astype(jnp.float32)  2.87 us
    rev x1, local copies, waits for them, and re-layouts, by_products(): lags = jnp.pad(jnp.flip(lags, 1), ((0, 0), (0, TILE)))  2.79 us
    add x1, other arithmetic, featurize(): summed + weights[offset] * extended[lag_rows - offset:lag_rows - offset +...  1.9 us
  transfers between devices with their start and end apart: 1, of which 0 were waited for; matrix products, arithmetic and copies ran while one was open for 5% of the time, Pallas kernels for 0%

commit v1 on v0

--- a/solution.py
+++ b/solution.py
@@ -168,18 +168,33 @@
 TILE = 256
 
 
+EDGE = 16
+
+
 def exchange_kernel(
-    query_ref,
-    kv_ref,
+    per_group,
+    own_ref,
+    taps_ref,
     lags_ref,
     gain_ref,
     out_ref,
+    halo_out,
+    halo_in,
+    lags_out,
+    lags_in,
+    lags_line,
+    query_out,
+    kv_out,
     query_rows,
     kv_rows,
     kv_seq,
     mixed_out,
     mixed_in,
     toeplitz,
+    halo_send,
+    halo_recv,
+    lags_send,
+    lags_recv,
     kv_send,
     kv_recv,
     query_send,
@@ -193,9 +208,9 @@
     blocks = lax.axis_size("ctx")
     my_chan = lax.axis_index("chan")
     my_block = lax.axis_index("ctx")
-    rows = kv_ref.shape[0]
+    rows = own_ref.shape[1]
     width = kv_rows.shape[1]
-    columns = kv_seq.shape[1]
+    length, columns = kv_seq.shape
     block_rows = rows * chans
 
     def other_chan(step):
@@ -203,35 +218,129 @@
 
     def other_block(step):
         return lax.rem(my_block + step + blocks, blocks)
+
+    def lanes(index, size):
+        return pl.ds(pl.multiple_of(index * size, size), size)
+
+    is_first = my_chan == 0
+    is_last = my_chan == chans - 1
+    previous = {"chan": other_chan(-1), "ctx": jnp.where(is_first, other_block(-1), my_block)}
+    following = {"chan": other_chan(1), "ctx": jnp.where(is_last, other_block(1), my_block)}
+    starts = jnp.logical_and(is_first, my_block == 0)
 
     barrier = pltpu.get_barrier_semaphore()
     for step in range(1, chans):
         pl.semaphore_signal(barrier, inc=1, device_id={"chan": other_chan(step)})
     for step in range(1, blocks):
         pl.semaphore_signal(barrier, inc=1, device_id={"ctx": other_block(step)})
-    pl.semaphore_wait(barrier, chans + blocks - 2)
-
-    def lanes(index, size):
-        return pl.ds(pl.multiple_of(index * size, size), size)
-
-    def over_chan(source, target, send, recv, step):
+    pl.semaphore_signal(barrier, inc=1, device_id=previous)
+
+    for part in range(3):
+        edge = own_ref[part, rows - EDGE :, :].astype(jnp.float32)
+        halo_out[2 * part : 2 * part + 2, :] = edge[EDGE - 2 :]
+    halo_out[6:8, :] = jnp.zeros((2, halo_out.shape[1]), jnp.float32)
+    span = lags_ref.shape[1]
+    across = lax.broadcasted_iota(jnp.int32, (span, span), 0)
+    down = lax.broadcasted_iota(jnp.int32, (span, span), 1)
+    flip = (across + down == span - 1).astype(jnp.bfloat16)
+    lags_out[...] = jnp.dot(
+        lags_ref[...].astype(jnp.bfloat16), flip, preferred_element_type=jnp.float32
+    )
+    lags_in[my_block] = lags_out[...]
+
+    piece = 256
+
+    def feature(part, count, here, with_halo):
+        value = own_ref[part, 0:count, here].astype(jnp.float32)
+        at = lax.broadcasted_iota(jnp.int32, value.shape, 0)
+        total = None
+        for offset in range(TAPS):
+            weight = taps_ref[offset, :, here].astype(jnp.float32)[part : part + 1]
+            moved = value
+            if offset:
+                moved = pltpu.roll(value, offset, 0)
+                if with_halo:
+                    for k in range(offset):
+                        row = 2 * part + 2 + k - offset
+                        edge = jnp.where(starts, 0.0, halo_in[row : row + 1, here])
+                        moved = jnp.where(at == k, edge, moved)
+            total = weight * moved if total is None else total + weight * moved
+        return total
+
+    def make_kv(target, at_row, count, chan, first_lane, with_halo):
+        @pl.loop(0, width // piece)
+        def _(index):
+            here = pl.ds(pl.multiple_of(chan * width + index * piece, piece), piece)
+            there = pl.ds(pl.multiple_of(first_lane + index * piece, piece), piece)
+            product = feature(1, count, here, with_halo) * feature(2, count, here, with_halo)
+            target[pl.ds(at_row, count), there] = product.astype(jnp.bfloat16)
+
+    def make_query(target, at_row, chan, first_lane):
+        @pl.loop(0, width // piece)
+        def _(index):
+            here = pl.ds(pl.multiple_of(chan * width + index * piece, piece), piece)
+            there = pl.ds(pl.multiple_of(first_lane + index * piece, piece), piece)
+            target[pl.ds(at_row, rows), there] = feature(0, rows, here, True).astype(jnp.bfloat16)
+
+    def over_chan(source, target, send, recv, step, first_row, count):
         to = other_chan(step)
+        there = pl.multiple_of(my_chan * rows + first_row, EDGE)
         return pltpu.make_async_remote_copy(
-            src_ref=source.at[:, lanes(to, width)],
-            dst_ref=target.at[lanes(my_chan, rows), :],
-            send_sem=send.at[step],
-            recv_sem=recv.at[step],
+            src_ref=source.at[pl.ds(first_row, count), lanes(to, width)],
+            dst_ref=target.at[pl.ds(there, count), :],
+            send_sem=send,
+            recv_sem=recv,
             device_id={"chan": to},
         )
 
-    kv_copies = [over_chan(kv_ref, kv_rows, kv_send, kv_recv, step) for step in range(1, chans)]
+    make_kv(kv_out, 0, rows, other_chan(1), other_chan(1) * width, False)
+    pl.semaphore_wait(barrier, chans + blocks - 1)
+
+    halo_copy = pltpu.make_async_remote_copy(
+        src_ref=halo_out,
+        dst_ref=halo_in,
+        send_sem=halo_send,
+        recv_sem=halo_recv,
+        device_id=following,
+    )
+    halo_copy.start()
+
+    low_copies = [
+        over_chan(kv_out, kv_rows, kv_send.at[0, k], kv_recv.at[0, k], k, EDGE, rows - EDGE)
+        for k in range(1, chans)
+    ]
+    edge_copies = [
+        over_chan(kv_out, kv_rows, kv_send.at[1, k], kv_recv.at[1, k], k, 0, EDGE)
+        for k in range(1, chans)
+    ]
     query_copies = [
-        over_chan(query_ref, query_rows, query_send, query_recv, step) for step in range(1, chans)
+        over_chan(query_out, query_rows, query_send.at[k], query_recv.at[k], k, 0, rows)
+        for k in range(1, chans)
     ]
-    for copy in kv_copies:
+    low_copies[0].start()
+    for step in range(2, chans):
+        to = other_chan(step)
+        make_kv(kv_out, 0, rows, to, to * width, False)
+        low_copies[step - 1].start()
+    lags_copies = []
+    for hop in range(1, blocks):
+        copy = pltpu.make_async_remote_copy(
+            src_ref=lags_out,
+            dst_ref=lags_in.at[my_block],
+            send_sem=lags_send.at[hop],
+            recv_sem=lags_recv.at[hop],
+            device_id={"ctx": other_block(hop)},
+        )
         copy.start()
-    kv_rows[lanes(my_chan, rows), :] = kv_ref[:, lanes(my_chan, width)]
-    query_rows[lanes(my_chan, rows), :] = query_ref[:, lanes(my_chan, width)]
+        lags_copies.append(copy)
+    my_rows = pl.multiple_of(my_chan * rows, rows)
+
+    halo_copy.wait_recv()
+    for step in range(1, chans):
+        to = other_chan(step)
+        make_kv(kv_out, 0, EDGE, to, to * width, True)
+        edge_copies[step - 1].start()
+    make_kv(kv_rows, my_rows, rows, my_chan, 0, True)
 
     seq_copies = []
 
@@ -253,20 +362,44 @@
         kv_seq[there, :] = kv_rows[here, lanes(my_block, columns)]
 
     forward(0)
-
-    toeplitz[0:TILE, :] = jnp.zeros((TILE, TILE), jnp.bfloat16)
-    length = kv_seq.shape[0]
-    for tile in range(length // TILE):
+    for step in range(1, chans):
+        to = other_chan(step)
+        make_query(query_out, 0, to, to * width)
+    make_query(query_rows, my_rows, my_chan, 0)
+
+    for copy in lags_copies:
+        copy.wait_recv()
+    group = my_block * columns // per_group
+    for block in range(blocks):
+        first = (blocks - 1 - block) * span
+        lags_line[:, first : first + span] = lags_in[block, pl.ds(group, 1), :]
+    lags_line[:, length:] = jnp.zeros((1, TILE), jnp.float32)
+
+    tiles = length // TILE
+    bands = block_rows // TILE
+    for tile in range(tiles):
         first = length - TILE - tile * TILE
-        window = jnp.broadcast_to(lags_ref[:, first : first + 2 * TILE], (TILE, 2 * TILE))
+        window = jnp.broadcast_to(lags_line[:, first : first + 2 * TILE], (TILE, 2 * TILE))
         turned = pltpu.roll(window, TILE + 1, 1, stride=1, stride_axis=0)
-        toeplitz[(tile + 1) * TILE : (tile + 2) * TILE, :] = turned[:, :TILE].astype(jnp.bfloat16)
+        turned = turned[:, :TILE].astype(jnp.bfloat16)
+        for band in range(bands):
+            column = tiles - bands + band - tile
+            if column >= 0:
+                toeplitz[
+                    band * TILE : (band + 1) * TILE, column * TILE : (column + 1) * TILE
+                ] = turned
+    for band in range(bands):
+        for column in range(tiles - bands + band + 1, tiles):
+            toeplitz[
+                band * TILE : (band + 1) * TILE, column * TILE : (column + 1) * TILE
+            ] = jnp.zeros((TILE, TILE), jnp.bfloat16)
 
     for step in range(1, chans):
-        kv_copies[step - 1].wait_recv()
+        low_copies[step - 1].wait_recv()
+        edge_copies[step - 1].wait_recv()
         forward(step)
-    for copy in query_copies:
-        copy.start()
+        low_copies[step - 1].wait_send()
+        query_copies[step - 1].start()
     for copy in seq_copies:
         copy.wait_recv()
 
@@ -284,13 +417,12 @@
 
     def convolve(block):
         def term(step, total):
-            later = block * block_rows - step * TILE + TILE
-            left = toeplitz[pl.ds(pl.multiple_of(later, TILE), block_rows), :]
-            right = kv_seq[lanes(step, TILE), :]
+            left = toeplitz[:, lanes(blocks - 1 - block + step, block_rows)]
+            right = kv_seq[lanes(step, block_rows), :]
             return total + jnp.dot(left, right, preferred_element_type=jnp.float32)
 
         start = jnp.zeros((block_rows, columns), jnp.float32)
-        total = lax.fori_loop(0, (block + 1) * (block_rows // TILE), term, start)
+        total = lax.fori_loop(0, block + 1, term, start)
         here = lanes(block, block_rows)
         mixed_out[here, :] = (total + gain * kv_seq[here, :].astype(jnp.float32)).astype(jnp.bfloat16)
 
@@ -315,53 +447,52 @@
     for hop in range(1, blocks):
         back_copies[hop - 1].wait_recv()
         gate(hop)
-    for copy in kv_copies + query_copies + seq_copies + back_copies:
+    for copy in edge_copies + query_copies + seq_copies + back_copies:
+        copy.wait_send()
+    for copy in lags_copies + [halo_copy]:
         copy.wait_send()
 
 
 def by_products(projected, short_taps, long_filter, skip_gain):
     chans = lax.axis_size("chan")
     blocks = lax.axis_size("ctx")
-    my_chan = lax.axis_index("chan")
     my_block = lax.axis_index("ctx")
-    own = projected[0]
-    rows, _, channels = own.shape
+    own = projected[0].transpose(1, 0, 2)
+    _, rows, channels = own.shape
     width = skip_gain.shape[0]
     columns = width // blocks
-    per_group = width // long_filter.shape[1]
+    groups, span = long_filter.shape[1], long_filter.shape[0]
     length = rows * chans * blocks
-    last = own[rows - (TAPS - 1) :]
-    pairs = []
-    for at in range(blocks * chans - 1):
-        source = (at % chans) * blocks + at // chans
-        after = at + 1
-        pairs.append((source, (after % chans) * blocks + after // chans))
-    earlier = lax.ppermute(last, ("chan", "ctx"), pairs)
-    queries, product = featurize(earlier, own, short_taps)
-
-    group = my_block * columns // per_group
-    lags = lax.all_gather(long_filter.T, "ctx", axis=1, tiled=True)
-    lags = lax.dynamic_slice_in_dim(lags, group, 1, 0)
-    lags = jnp.pad(jnp.flip(lags, 1), ((0, 0), (0, TILE)))
     gains = lax.dynamic_slice_in_dim(skip_gain, my_block * columns, columns, 0)[None]
 
     block_rows = rows * chans
     vmem = pl.BlockSpec(memory_space=pltpu.VMEM)
     dma = pltpu.SemaphoreType.DMA
     return pl.pallas_call(
-        exchange_kernel,
+        functools.partial(exchange_kernel, width // groups),
         out_shape=jax.ShapeDtypeStruct((block_rows, width), jnp.bfloat16),
         in_specs=[vmem] * 4,
         out_specs=vmem,
         scratch_shapes=[
+            pltpu.VMEM((8, channels), jnp.float32),
+            pltpu.VMEM((8, channels), jnp.float32),
+            pltpu.VMEM((groups, span), jnp.float32),
+            pltpu.VMEM((blocks, groups, span), jnp.float32),
+            pltpu.VMEM((1, length + TILE), jnp.float32),
+            pltpu.VMEM((rows, channels), jnp.bfloat16),
+            pltpu.VMEM((rows, channels), jnp.bfloat16),
             pltpu.VMEM((block_rows, width), jnp.bfloat16),
             pltpu.VMEM((block_rows, width), jnp.bfloat16),
             pltpu.VMEM((length, columns), jnp.bfloat16),
             pltpu.VMEM((length, columns), jnp.bfloat16),
             pltpu.VMEM((block_rows, width), jnp.bfloat16),
-            pltpu.VMEM((length + TILE, TILE), jnp.bfloat16),
-            dma((chans,)),
-            dma((chans,)),
+            pltpu.VMEM((block_rows, length), jnp.bfloat16),
+            dma(()),
+            dma(()),
+            dma((blocks,)),
+            dma((blocks,)),
+            dma((2, chans)),
+            dma((2, chans)),
             dma((chans,)),
             dma((chans,)),
             dma((chans, blocks)),
@@ -370,9 +501,9 @@
             dma((blocks,)),
         ],
         compiler_params=pltpu.CompilerParams(
-            collective_id=0, has_side_effects=True, vmem_limit_bytes=40 * 1024 * 1024
+            collective_id=0, has_side_effects=True, vmem_limit_bytes=48 * 1024 * 1024
         ),
-    )(queries, product, lags, gains)
+    )(own, short_taps, long_filter.T, gains)
 
 
 def local(projected, short_taps, long_filter, skip_gain):
@@ -383,7 +514,8 @@
     columns = width // blocks
     per_group = width // long_filter.shape[1]
     fits = columns % 128 == 0 and per_group % columns == 0
-    fits = fits and rows % 16 == 0 and rows * chans % TILE == 0
+    fits = fits and rows % 32 == 0 and rows * chans % TILE == 0 and width % 256 == 0
+    fits = fits and per_group % 128 == 0
     if fits:
         return by_products(projected, short_taps, long_filter, skip_gain)
     return by_transform(projected, short_taps, long_filter, skip_gain)

time: 80.2 us -> 74 us (0.923)
  the two profiles are of different devices: /device:TPU:31 before, /device:TPU:7 now
where the time goes in v1:
time: 74 us; the launch traced here: 73.7 us
  Pallas kernels  68.5 us (93%)
  local copies, waits for them, and re-layouts  5.21 us (7%)
    pallas_call x1, Pallas kernels, by_products(): pl.pallas_call(functools.partial(exchange_kernel, width // groups), out_s...  68.5 us
    unnamed x9, local copies, waits for them, and re-layouts  5.14 us

profile of v1, /device:TPU:7, one launch (start us, length us, event | category | flops | bytes accessed | tf_op | source)
XLA Modules:
  0.0 73.7 jit_solution(10886220157445629171)
XLA Ops:
  0.0 0.0 copy-start
  0.0 0.7 copy-done
  0.7 0.1 dynamic-slice_bitcast_fusion.gain_ref
  0.8 0.0 copy-start.1
  0.8 1.9 %copy-done.1 = bf16[1,128,3,4096]{3,1,2,0:T(8,128)(2,1)S(1)} copy-done((bf16[1,128,3,4096]{3,1,2,0:T(8,128)(2,1)S(1)}, bf16[1,128,3,4096]{3,1,2,0:T(8,128)(2,1)}, u32[]{:S(2)}) %copy-start.1) | copy-done | bytes 3145752
  2.7 0.0 copy-start.2
  2.7 0.9 %copy-done.2 = bf16[3,3,4096]{2,1,0:T(4,128)(2,1)S(1)} copy-done((bf16[3,3,4096]{2,1,0:T(4,128)(2,1)S(1)}, bf16[3,3,4096]{2,1,0:T(4,128)(2,1)}, u32[]{:S(2)}) %copy-start.2) | copy-done | bytes 73752
  3.5 0.0 copy-start.3
  3.5 0.7 copy-done.3
  4.2 68.5 %shard_map.46 = bf16[512,1024]{1,0:T(8,128)(2,1)S(1)} custom-call(bf16[3,128,4096]{2,1,0:T(8,128)(2,1)S(1)} %bitcast.6, bf16[3,3,4096]{2,1,0:T(4,128)(2,1)S(1)} %copy-done.2, f32[4,512]{1,0:T(4,128)S(1)} %bitcast.7, f32[1,128]{1,0:T(1,128)S(1)} %dynamic-slice_bitcast_fusion.gain_ref), custom_call_target="tpu_custom_call" | custom-call | tf_op jit(solution)/shard_map/pallas_call | solution.py:471
  72.8 1.0 %copy.6 = bf16[512,1024]{1,0:T(8,128)(2,1)} copy(bf16[512,1024]{1,0:T(8,128)(2,1)S(1)} %shard_map.46) | data formatting | bytes 2097152
Async XLA Ops:
  0.0 0.7 copy-start
  0.8 1.9 %copy-start.1 = (bf16[1,128,3,4096]{3,1,2,0:T(8,128)(2,1)S(1)}, bf16[1,128,3,4096]{3,1,2,0:T(8,128)(2,1)}, u32[]{:S(2)}) copy-start(bf16[1,128,3,4096]{3,1,2,0:T(8,128)(2,1)} %param.4) | copy-start | bytes 9437188
  2.7 0.9 %copy-start.2 = (bf16[3,3,4096]{2,1,0:T(4,128)(2,1)S(1)}, bf16[3,3,4096]{2,1,0:T(4,128)(2,1)}, u32[]{:S(2)}) copy-start(bf16[3,3,4096]{2,1,0:T(4,128)(2,1)} %taps_ref.1) | copy-start | bytes 221188
  3.5 0.7 copy-start.3

commit v2 on v1

--- a/solution.py
+++ b/solution.py
@@ -166,6 +166,8 @@
 
 
 TILE = 256
+PIECES = 4
+AHEAD = 2
 
 
 EDGE = 16
@@ -313,10 +315,27 @@
         over_chan(kv_out, kv_rows, kv_send.at[1, k], kv_recv.at[1, k], k, 0, EDGE)
         for k in range(1, chans)
     ]
-    query_copies = [
-        over_chan(query_out, query_rows, query_send.at[k], query_recv.at[k], k, 0, rows)
-        for k in range(1, chans)
-    ]
+    slab = width // PIECES
+
+    def query_piece(index, step):
+        to = other_chan(step)
+        lane = pl.multiple_of(to * width + index * slab, slab)
+        return pltpu.make_async_remote_copy(
+            src_ref=query_out.at[:, pl.ds(lane, slab)],
+            dst_ref=query_rows.at[lanes(my_chan, rows), index * slab : (index + 1) * slab],
+            send_sem=query_send.at[index, step],
+            recv_sem=query_recv.at[index, step],
+            device_id={"chan": to},
+        )
+
+    query_copies = [[query_piece(i, k) for k in range(1, chans)] for i in range(PIECES)]
+    waiting = list(query_copies)
+
+    def send_queries(count):
+        for _ in range(min(count, len(waiting))):
+            for copy in waiting.pop(0):
+                copy.start()
+
     low_copies[0].start()
     for step in range(2, chans):
         to = other_chan(step)
@@ -399,7 +418,7 @@
         edge_copies[step - 1].wait_recv()
         forward(step)
         low_copies[step - 1].wait_send()
-        query_copies[step - 1].start()
+    send_queries(AHEAD)
     for copy in seq_copies:
         copy.wait_recv()
 
@@ -409,7 +428,7 @@
         to = other_block(hop)
         return pltpu.make_async_remote_copy(
             src_ref=mixed_out.at[lanes(to, block_rows), :],
-            dst_ref=mixed_in.at[:, lanes(my_block, columns)],
+            dst_ref=mixed_in.at[my_block],
             send_sem=back_send.at[hop],
             recv_sem=back_recv.at[hop],
             device_id={"ctx": to},
@@ -432,15 +451,18 @@
         copy = returning(hop)
         copy.start()
         back_copies.append(copy)
+        send_queries(1)
+    send_queries(PIECES)
     convolve(my_block)
-    mixed_in[:, lanes(my_block, columns)] = mixed_out[lanes(my_block, block_rows), :]
-
+    mixed_in[my_block] = mixed_out[lanes(my_block, block_rows), :]
+
+    query_copies = [copy for each in query_copies for copy in each]
     for copy in query_copies:
         copy.wait_recv()
 
     def gate(hop):
         here = lanes(other_block(-hop), columns)
-        product = query_rows[:, here].astype(jnp.float32) * mixed_in[:, here].astype(jnp.float32)
+        product = query_rows[:, here].astype(jnp.float32) * mixed_in[other_block(-hop)].astype(jnp.float32)
         out_ref[:, here] = product.astype(jnp.bfloat16)
 
     gate(0)
@@ -485,7 +507,7 @@
             pltpu.VMEM((block_rows, width), jnp.bfloat16),
             pltpu.VMEM((length, columns), jnp.bfloat16),
             pltpu.VMEM((length, columns), jnp.bfloat16),
-            pltpu.VMEM((block_rows, width), jnp.bfloat16),
+            pltpu.VMEM((blocks, block_rows, columns), jnp.bfloat16),
             pltpu.VMEM((block_rows, length), jnp.bfloat16),
             dma(()),
             dma(()),
@@ -493,8 +515,8 @@
             dma((blocks,)),
             dma((2, chans)),
             dma((2, chans)),
-            dma((chans,)),
-            dma((chans,)),
+            dma((PIECES, chans)),
+            dma((PIECES, chans)),
             dma((chans, blocks)),
             dma((chans, blocks)),
             dma((blocks,)),

time: 74 us -> 62.9 us (0.85)
  Pallas kernels: 68.5 us -> 57.4 us
    pallas_call x1, Pallas kernels: 68.5 us -> 57.4 us  [by_products(): pl.pallas_call(functools.partial(exchange_kernel, width // groups), out_s...]
where the time goes in v2:
time: 62.9 us; the launch traced here: 62.6 us
  Pallas kernels  57.4 us (91%)
  local copies, waits for them, and re-layouts  5.21 us (8%)
    pallas_call x1, Pallas kernels, by_products(): pl.pallas_call(functools.partial(exchange_kernel, width // groups), out_s...  57.4 us
    unnamed x9, local copies, waits for them, and re-layouts  5.14 us

profile of v2, /device:TPU:7, one launch (start us, length us, event | category | flops | bytes accessed | tf_op | source)
XLA Modules:
  0.0 62.6 jit_solution(2943196300924226097)
XLA Ops:
  0.0 0.0 copy-start
  0.0 0.7 %copy-done = f32[1024]{0:T(1024)S(1)} copy-done((f32[1024]{0:T(1024)S(1)}, f32[1024]{0:T(1024)}, u32[]{:S(2)}) %copy-start) | copy-done | bytes 4120
  0.7 0.1 dynamic-slice_bitcast_fusion.gain_ref
  0.8 0.0 copy-start.1
  0.8 1.9 %copy-done.1 = bf16[1,128,3,4096]{3,1,2,0:T(8,128)(2,1)S(1)} copy-done((bf16[1,128,3,4096]{3,1,2,0:T(8,128)(2,1)S(1)}, bf16[1,128,3,4096]{3,1,2,0:T(8,128)(2,1)}, u32[]{:S(2)}) %copy-start.1) | copy-done | bytes 3145752
  2.7 0.0 copy-start.2
  2.7 0.9 %copy-done.2 = bf16[3,3,4096]{2,1,0:T(4,128)(2,1)S(1)} copy-done((bf16[3,3,4096]{2,1,0:T(4,128)(2,1)S(1)}, bf16[3,3,4096]{2,1,0:T(4,128)(2,1)}, u32[]{:S(2)}) %copy-start.2) | copy-done | bytes 73752
  3.5 0.0 copy-start.3
  3.5 0.7 %copy-done.3 = f32[512,4]{0,1:T(4,128)S(1)} copy-done((f32[512,4]{0,1:T(4,128)S(1)}, f32[512,4]{0,1:T(4,128)}, u32[]{:S(2)}) %copy-start.3) | copy-done | bytes 8216
  4.2 57.4 %shard_map.46 = bf16[512,1024]{1,0:T(8,128)(2,1)S(1)} custom-call(bf16[3,128,4096]{2,1,0:T(8,128)(2,1)S(1)} %bitcast.6, bf16[3,3,4096]{2,1,0:T(4,128)(2,1)S(1)} %copy-done.2, f32[4,512]{1,0:T(4,128)S(1)} %bitcast.7, f32[1,128]{1,0:T(1,128)S(1)} %dynamic-slice_bitcast_fusion.gain_ref), custom_call_target="tpu_custom_call" | custom-call | tf_op jit(solution)/shard_map/pallas_call | solution.py:493
  61.7 1.0 %copy.6 = bf16[512,1024]{1,0:T(8,128)(2,1)} copy(bf16[512,1024]{1,0:T(8,128)(2,1)S(1)} %shard_map.46) | data formatting | bytes 2097152
Async XLA Ops:
  0.0 0.7 %copy-start = (f32[1024]{0:T(1024)S(1)}, f32[1024]{0:T(1024)}, u32[]{:S(2)}) copy-start(f32[1024]{0:T(1024)} %param.7) | copy-start | bytes 12292
  0.8 1.9 %copy-start.1 = (bf16[1,128,3,4096]{3,1,2,0:T(8,128)(2,1)S(1)}, bf16[1,128,3,4096]{3,1,2,0:T(8,128)(2,1)}, u32[]{:S(2)}) copy-start(bf16[1,128,3,4096]{3,1,2,0:T(8,128)(2,1)} %param.4) | copy-start | bytes 9437188
  2.7 0.9 %copy-start.2 = (bf16[3,3,4096]{2,1,0:T(4,128)(2,1)S(1)}, bf16[3,3,4096]{2,1,0:T(4,128)(2,1)}, u32[]{:S(2)}) copy-start(bf16[3,3,4096]{2,1,0:T(4,128)(2,1)} %taps_ref.1) | copy-start | bytes 221188
  3.5 0.7 %copy-start.3 = (f32[512,4]{0,1:T(4,128)S(1)}, f32[512,4]{0,1:T(4,128)}, u32[]{:S(2)}) copy-start(f32[512,4]{0,1:T(4,128)} %param.6) | copy-start | bytes 24580

commit v3 on v2

--- a/solution.py
+++ b/solution.py
@@ -168,6 +168,7 @@
 TILE = 256
 PIECES = 4
 AHEAD = 2
+EARLY = 1
 
 
 EDGE = 16
@@ -180,6 +181,7 @@
     lags_ref,
     gain_ref,
     out_ref,
+    halo_line,
     halo_out,
     halo_in,
     lags_out,
@@ -239,8 +241,11 @@
 
     for part in range(3):
         edge = own_ref[part, rows - EDGE :, :].astype(jnp.float32)
-        halo_out[2 * part : 2 * part + 2, :] = edge[EDGE - 2 :]
-    halo_out[6:8, :] = jnp.zeros((2, halo_out.shape[1]), jnp.float32)
+        halo_line[2 * part : 2 * part + 2, :] = edge[EDGE - 2 :]
+    halo_line[6:8, :] = jnp.zeros((2, halo_line.shape[1]), jnp.float32)
+    half = halo_out.shape[1]
+    halves = [halo_line[:, :half], halo_line[:, half:]]
+    halo_out[...] = jnp.concatenate(halves, axis=0).astype(jnp.bfloat16)
     span = lags_ref.shape[1]
     across = lax.broadcasted_iota(jnp.int32, (span, span), 0)
     down = lax.broadcasted_iota(jnp.int32, (span, span), 1)
@@ -264,7 +269,7 @@
                 if with_halo:
                     for k in range(offset):
                         row = 2 * part + 2 + k - offset
-                        edge = jnp.where(starts, 0.0, halo_in[row : row + 1, here])
+                        edge = jnp.where(starts, 0.0, halo_line[row : row + 1, here])
                         moved = jnp.where(at == k, edge, moved)
             total = weight * moved if total is None else total + weight * moved
         return total
@@ -355,6 +360,9 @@
     my_rows = pl.multiple_of(my_chan * rows, rows)
 
     halo_copy.wait_recv()
+    arrived = halo_in[...].astype(jnp.float32)
+    halo_line[:, :half] = arrived[:8]
+    halo_line[:, half:] = arrived[8:]
     for step in range(1, chans):
         to = other_chan(step)
         make_kv(kv_out, 0, EDGE, to, to * width, True)
@@ -414,11 +422,13 @@
             ] = jnp.zeros((TILE, TILE), jnp.bfloat16)
 
     for step in range(1, chans):
+        if step == chans - 1:
+            send_queries(EARLY)
         low_copies[step - 1].wait_recv()
         edge_copies[step - 1].wait_recv()
         forward(step)
         low_copies[step - 1].wait_send()
-    send_queries(AHEAD)
+    send_queries(AHEAD - EARLY)
     for copy in seq_copies:
         copy.wait_recv()
 
@@ -456,19 +466,17 @@
     convolve(my_block)
     mixed_in[my_block] = mixed_out[lanes(my_block, block_rows), :]
 
+    for copy in back_copies:
+        copy.wait_recv()
+    for index in range(PIECES):
+        for copy in query_copies[index]:
+            copy.wait_recv()
+        for at in range(index * slab, (index + 1) * slab, columns):
+            here = slice(at, at + columns)
+            mixed = mixed_in[at // columns].astype(jnp.float32)
+            product = query_rows[:, here].astype(jnp.float32) * mixed
+            out_ref[:, here] = product.astype(jnp.bfloat16)
     query_copies = [copy for each in query_copies for copy in each]
-    for copy in query_copies:
-        copy.wait_recv()
-
-    def gate(hop):
-        here = lanes(other_block(-hop), columns)
-        product = query_rows[:, here].astype(jnp.float32) * mixed_in[other_block(-hop)].astype(jnp.float32)
-        out_ref[:, here] = product.astype(jnp.bfloat16)
-
-    gate(0)
-    for hop in range(1, blocks):
-        back_copies[hop - 1].wait_recv()
-        gate(hop)
     for copy in edge_copies + query_copies + seq_copies + back_copies:
         copy.wait_send()
     for copy in lags_copies + [halo_copy]:
@@ -497,7 +505,8 @@
         out_specs=vmem,
         scratch_shapes=[
             pltpu.VMEM((8, channels), jnp.float32),
-            pltpu.VMEM((8, channels), jnp.float32),
+            pltpu.VMEM((16, channels // 2), jnp.bfloat16),
+            pltpu.VMEM((16, channels // 2), jnp.bfloat16),
             pltpu.VMEM((groups, span), jnp.float32),
             pltpu.VMEM((blocks, groups, span), jnp.float32),
             pltpu.VMEM((1, length + TILE), jnp.float32),
@@ -537,7 +546,7 @@
     per_group = width // long_filter.shape[1]
     fits = columns % 128 == 0 and per_group % columns == 0
     fits = fits and rows % 32 == 0 and rows * chans % TILE == 0 and width % 256 == 0
-    fits = fits and per_group % 128 == 0
+    fits = fits and per_group % 128 == 0 and width // PIECES % columns == 0
     if fits:
         return by_products(projected, short_taps, long_filter, skip_gain)
     return by_transform(projected, short_taps, long_filter, skip_gain)

time: 62.9 us -> 61.7 us (0.981)
  Pallas kernels: 57.4 us -> 56.2 us
    pallas_call x1, Pallas kernels: 57.4 us -> 56.2 us  [by_products(): pl.pallas_call(functools.partial(exchange_kernel, width // groups), out_s...]
where the time goes in v3:
time: 61.7 us; the launch traced here: 61.4 us
  Pallas kernels  56.2 us (91%)
  local copies, waits for them, and re-layouts  5.21 us (8%)
    pallas_call x1, Pallas kernels, by_products(): pl.pallas_call(functools.partial(exchange_kernel, width // groups), out_s...  56.2 us
    unnamed x9, local copies, waits for them, and re-layouts  5.14 us

profile of v3, /device:TPU:7, one launch (start us, length us, event | category | flops | bytes accessed | tf_op | source)
XLA Modules:
  0.0 61.4 jit_solution(12183084569915484217)
XLA Ops:
  0.0 0.0 copy-start
  0.0 0.7 %copy-done = f32[1024]{0:T(1024)S(1)} copy-done((f32[1024]{0:T(1024)S(1)}, f32[1024]{0:T(1024)}, u32[]{:S(2)}) %copy-start) | copy-done | bytes 4120
  0.7 0.1 dynamic-slice_bitcast_fusion.gain_ref
  0.8 0.0 copy-start.1
  0.8 1.9 %copy-done.1 = bf16[1,128,3,4096]{3,1,2,0:T(8,128)(2,1)S(1)} copy-done((bf16[1,128,3,4096]{3,1,2,0:T(8,128)(2,1)S(1)}, bf16[1,128,3,4096]{3,1,2,0:T(8,128)(2,1)}, u32[]{:S(2)}) %copy-start.1) | copy-done | bytes 3145752
  2.7 0.0 copy-start.2
  2.7 0.9 %copy-done.2 = bf16[3,3,4096]{2,1,0:T(4,128)(2,1)S(1)} copy-done((bf16[3,3,4096]{2,1,0:T(4,128)(2,1)S(1)}, bf16[3,3,4096]{2,1,0:T(4,128)(2,1)}, u32[]{:S(2)}) %copy-start.2) | copy-done | bytes 73752
  3.5 0.0 copy-start.3
  3.5 0.7 %copy-done.3 = f32[512,4]{0,1:T(4,128)S(1)} copy-done((f32[512,4]{0,1:T(4,128)S(1)}, f32[512,4]{0,1:T(4,128)}, u32[]{:S(2)}) %copy-start.3) | copy-done | bytes 8216
  4.2 56.2 %shard_map.46 = bf16[512,1024]{1,0:T(8,128)(2,1)S(1)} custom-call(bf16[3,128,4096]{2,1,0:T(8,128)(2,1)S(1)} %bitcast.6, bf16[3,3,4096]{2,1,0:T(4,128)(2,1)S(1)} %copy-done.2, f32[4,512]{1,0:T(4,128)S(1)} %bitcast.7, f32[1,128]{1,0:T(1,128)S(1)} %dynamic-slice_bitcast_fusion.gain_ref), custom_call_target="tpu_custom_call" | custom-call | tf_op jit(solution)/shard_map/pallas_call | solution.py:501
  60.5 1.0 %copy.6 = bf16[512,1024]{1,0:T(8,128)(2,1)} copy(bf16[512,1024]{1,0:T(8,128)(2,1)S(1)} %shard_map.46) | data formatting | bytes 2097152
Async XLA Ops:
  0.0 0.7 %copy-start = (f32[1024]{0:T(1024)S(1)}, f32[1024]{0:T(1024)}, u32[]{:S(2)}) copy-start(f32[1024]{0:T(1024)} %param.7) | copy-start | bytes 12292
  0.8 1.9 %copy-start.1 = (bf16[1,128,3,4096]{3,1,2,0:T(8,128)(2,1)S(1)}, bf16[1,128,3,4096]{3,1,2,0:T(8,128)(2,1)}, u32[]{:S(2)}) copy-start(bf16[1,128,3,4096]{3,1,2,0:T(8,128)(2,1)} %param.4) | copy-start | bytes 9437188
  2.7 0.9 %copy-start.2 = (bf16[3,3,4096]{2,1,0:T(4,128)(2,1)S(1)}, bf16[3,3,4096]{2,1,0:T(4,128)(2,1)}, u32[]{:S(2)}) copy-start(bf16[3,3,4096]{2,1,0:T(4,128)(2,1)} %taps_ref.1) | copy-start | bytes 221188
  3.5 0.7 %copy-start.3 = (f32[512,4]{0,1:T(4,128)S(1)}, f32[512,4]{0,1:T(4,128)}, u32[]{:S(2)}) copy-start(f32[512,4]{0,1:T(4,128)} %param.6) | copy-start | bytes 24580
